TPU v7x, 256 devices: a whole 4x4x8 slice. The times are simulated.
256 devices in a mesh: blk: 8 (over x_hi, y), wide: 32 (over x_lo, z, core).
Axes of the slice: x: 4 (x_hi: 2, x_lo: 2; x = x_hi * 2 + x_lo), y: 4, z: 8, core: 2. Of those that a mesh axis runs over, the one named last changes fastest.
Arguments:
- users: bfloat16 [1048576, 256], P(('blk', 'wide')), may hold values from -1.5 to 1.5
- items: bfloat16 [131072, 256], P(('blk', 'wide')), may hold values from -1.5 to 1.5
- user_pairs: int32 [256, 8, 16], P(('blk', 'wide')), may hold values from 0 to 127, as said below
- user_ratings: bfloat16 [256, 8, 16, 128, 128], P(('blk', 'wide')), may hold values from 0 to 5, as said below
- user_counts: int32 [256, 8], P(('blk', 'wide')), may hold values from 1 to 16
- item_pairs: int32 [256, 128], P(('blk', 'wide')), may hold values from 0 to 127, as said below
- item_ratings: bfloat16 [256, 128, 128, 128], P(('blk', 'wide')), may hold values from 0 to 5, as said below
- live_item_counts: int32 [256], P(('blk', 'wide')), may hold values from 1 to 128
Outputs:
- new_users: bfloat16 [1048576, 256], P(('blk', 'wide'))
- new_items: bfloat16 [131072, 256], P(('blk', 'wide'))
Inputs may be any that keep to these rules, and one draw needn't show every extreme that they name: `user_pairs`: within one group and slice the slots name distinct pairs; p // 4 is the user block, p % (4) the item block. `user_ratings`: 0 marks an unobserved rating; observed ratings lie in 1 to 5. `item_pairs`: within one group the slots name distinct pairs; p // 32 is the item block, p % (32) the relaid user block. `item_ratings`: 0 marks an unobserved rating; observed ratings lie in 1 to 5.
All inputs are finite; a program needn't handle non-finite values.
Results may differ from a plain program's by a relative error of at most 0.0044.
Values may be sent and summed in bfloat16 or wider, within the bound.
A program may use at most 128 MiB of HBM per device.

v0:
```python
import jax
import jax.numpy as jnp
from jax import lax
from jax.sharding import PartitionSpec as P

user_rate = 0.03
item_rate = 0.005
shrink = 0.05


def from_behind(value, axis, steps):
    count = lax.axis_size(axis)
    pairs = [(source, (source + steps) % count) for source in range(count)]
    return lax.ppermute(value, axis, pairs)


def block_loss_terms(row_factor_matrix, column_factor_matrix, ratings, slot_live):
    predicted_rating = jnp.einsum(
        "tgo,tco->tgc", row_factor_matrix, column_factor_matrix, preferred_element_type=jnp.float32
    )
    observed = (ratings != 0) & slot_live[:, None, None]
    rating_error = jnp.where(
        observed, ratings.astype(jnp.float32) - predicted_rating, jnp.float32(0.0)
    ).astype(jnp.bfloat16)
    return jnp.einsum(
        "yvg,ygt->yvt", rating_error, column_factor_matrix, preferred_element_type=jnp.float32
    )


def collect(terms, block_index, count_of_blocks):
    return jax.ops.segment_sum(terms, block_index, num_segments=count_of_blocks)


def per_device(
    users, items, user_pairs, user_ratings, user_counts, item_pairs, item_ratings, live_item_counts
):
    rank_width = users.shape[1]
    block_size = user_ratings.shape[-1]
    own_users = users.reshape(-1, block_size, rank_width)
    user_blocks = own_users.shape[0]
    item_rows = items.shape[0]
    item_rating_blocks = item_rows // block_size
    loop_size = lax.axis_size("blk")
    slice_place = lax.axis_index("blk")
    pairs_all = user_pairs[0]
    ratings_all = user_ratings[0]
    counts_all = user_counts[0]
    slot_total = pairs_all.shape[1]
    user_total = jnp.zeros((user_blocks, block_size, rank_width), jnp.float32)
    held_items = items
    for offset in range(loop_size):
        if offset > 0:
            held_items = from_behind(held_items, "blk", 1)
        source = (slice_place - offset) % loop_size
        visit_slot_pairs = lax.dynamic_index_in_dim(pairs_all, source, 0, keepdims=False)
        slot_ratings = lax.dynamic_index_in_dim(ratings_all, source, 0, keepdims=False)
        live_count = lax.dynamic_index_in_dim(counts_all, source, 0, keepdims=False)
        visit_user_index = visit_slot_pairs // item_rating_blocks
        visit_item_index = visit_slot_pairs % item_rating_blocks
        column_factor_matrix = held_items.reshape(item_rating_blocks, block_size, rank_width)[
            visit_item_index
        ]
        row_factor_matrix = own_users[visit_user_index]
        visit_slot_live = jnp.arange(slot_total, dtype=jnp.int32) < live_count
        visit_terms = block_loss_terms(
            row_factor_matrix, column_factor_matrix, slot_ratings, visit_slot_live
        )
        user_total = user_total + collect(visit_terms, visit_user_index, user_blocks)
    old_users = users.astype(jnp.float32)
    new_users = (
        old_users + user_rate * (user_total.reshape(old_users.shape) - shrink * old_users)
    ).astype(jnp.bfloat16)
    relaid = lax.all_to_all(new_users, "wide", split_axis=0, concat_axis=0, tiled=True)
    users_here = relaid.reshape(user_blocks, block_size, rank_width)
    own_items = items.reshape(item_rating_blocks, block_size, rank_width)
    slot_pairs = item_pairs[0]
    item_index = slot_pairs // user_blocks
    user_index = slot_pairs % user_blocks
    slot_live = jnp.arange(slot_pairs.shape[0], dtype=jnp.int32) < live_item_counts[0]
    terms = block_loss_terms(
        own_items[item_index], users_here[user_index], item_ratings[0], slot_live
    )
    item_total = collect(terms, item_index, item_rating_blocks)
    old_items = items.astype(jnp.float32)
    new_items = (
        old_items + item_rate * (item_total.reshape(old_items.shape) - shrink * old_items)
    ).astype(jnp.bfloat16)
    return (new_users, new_items)


def solution(mesh):
    return jax.shard_map(
        per_device,
        mesh=mesh,
        in_specs=(
            P(("blk", "wide"), None),
            P(("blk", "wide"), None),
            P(("blk", "wide"), None, None),
            P(("blk", "wide"), None, None, None, None),
            P(("blk", "wide"), None),
            P(("blk", "wide"), None),
            P(("blk", "wide"), None, None, None),
            P(("blk", "wide")),
        ),
        out_specs=(P(("blk", "wide"), None), P(("blk", "wide"), None)),
        check_vma=False,
    )
```

profile of v0, /device:TPU:11, one launch (start us, length us, event | category | flops | bytes accessed | tf_op | source)
XLA Modules:
  0.0 259.6 jit_solution(14728638072072051250)
XLA Ops:
  0.6 1.4 collective-permute-start
  2.0 1.0 fusion.118
  3.1 1.6 constant_dynamic-slice_fusion
  4.7 0.6 iota_compare_fusion.7
  5.4 0.6 iota_compare_fusion.8
  6.0 0.6 iota_compare_fusion.6
  7.3 0.7 iota_compare_fusion.4
  8.1 0.7 iota_compare_fusion.3
  8.8 0.6 iota_compare_fusion.2
  9.4 1.6 gather_fusion.1
  11.0 3.3 %gather_fusion = bf16[16,128,256]{2,1,0:T(8,128)(2,1)} fusion(bf16[32,128,256]{2,1,0:T(8,128)(2,1)} %bitcast.277, s32[1024]{0:T(1024)S(1)} %pad_clamp_fusion.17), kind=kCustom, calls=%fused_computation | custom fusion | bytes 2097216 | tf_op jit(solution)/shard_map/gather | solution.py:63
  14.4 3.4 %fusion.36 = f32[16,128,256]{2,1,0:T(8,128)} fusion(bf16[16,128,256]{2,1,0:T(8,128)(2,1)S(1)} %gather_fusion.1, bf16[16,128,256]{2,1,0:T(8,128)(2,1)} %gather_fusion, bf16[1,8,16,128,128]{4,3,2,1,0:T(8,128)(2,1)} %param.11, s32[]{:T(128)S(6)} %select_n.521, pred[16]{0:T(512)(128)(4,1)S(1)} %iota_compare_fusion.8), kind=kOutput, calls=%fused_computation.73 | convolution fusion | flops 270532608 | bytes 5767684 | tf_op jit(solution)/shard_map/yvg,ygt->yvt/dot_general | solution.py:25
  17.8 0.6 iota_compare_fusion.1
  18.4 1.6 gather_fusion.2
  20.0 1.6 gather_fusion.4
  21.7 1.6 gather_fusion.6
  23.3 1.6 gather_fusion.8
  24.9 1.6 gather_fusion.10
  26.5 1.6 gather_fusion.12
  28.1 1.7 gather_fusion.14
  29.7 2.5 broadcast.1283.clone
  32.2 5.2 %scatter_fusion = f32[32,128,256]{2,1,0:T(8,128)} fusion(f32[32,128,256]{2,1,0:T(8,128)} %broadcast.1283.clone, s32[16]{0:T(128)S(1)} %bitcast.297, f32[16,128,256]{2,1,0:T(8,128)} %fusion.36), kind=kCustom, calls=%fused_computation.18 | custom fusion | flops 524288 | bytes 6291520 | tf_op jit(solution)/shard_map/scatter-add | solution.py:31
  37.4 0.6 gather_fusion.3
  38.0 1.2 collective-permute-start.1
  39.3 3.4 %fusion.35 = f32[16,128,256]{2,1,0:T(8,128)} fusion(bf16[16,128,256]{2,1,0:T(8,128)(2,1)S(1)} %gather_fusion.3, bf16[16,128,256]{2,1,0:T(8,128)(2,1)} %gather_fusion.2, bf16[1,8,16,128,128]{4,3,2,1,0:T(8,128)(2,1)} %param.11, s32[]{:T(128)S(6)} %select_n.528, pred[16]{0:T(512)(128)(4,1)S(1)} %iota_compare_fusion.7), kind=kOutput, calls=%fused_computation.72 | convolution fusion | flops 270532608 | bytes 5767684 | tf_op jit(solution)/shard_map/yvg,ygt->yvt/dot_general | solution.py:25
  42.7 2.5 broadcast.1283.clone.1
  45.2 5.3 %scatter_fusion.1 = f32[32,128,256]{2,1,0:T(8,128)} fusion(f32[32,128,256]{2,1,0:T(8,128)} %broadcast.1283.clone.1, s32[16]{0:T(128)S(1)} %bitcast.296, f32[16,128,256]{2,1,0:T(8,128)} %fusion.35), kind=kCustom, calls=%fused_computation.19 | custom fusion | flops 524288 | bytes 6291520 | tf_op jit(solution)/shard_map/scatter-add | solution.py:31
  50.5 6.1 %add.522 = f32[32,128,256]{2,1,0:T(8,128)} add(f32[32,128,256]{2,1,0:T(8,128)} %scatter_fusion, f32[32,128,256]{2,1,0:T(8,128)} %scatter_fusion.1) | non-fusion elementwise | flops 1048576 | bytes 12582912 | tf_op jit(solution)/shard_map/add | solution.py:68
  56.6 1.6 gather_fusion.5
  58.2 1.4 collective-permute-start.2
  59.6 3.4 %fusion.34 = f32[16,128,256]{2,1,0:T(8,128)} fusion(bf16[16,128,256]{2,1,0:T(8,128)(2,1)S(1)} %gather_fusion.5, bf16[16,128,256]{2,1,0:T(8,128)(2,1)} %gather_fusion.4, bf16[1,8,16,128,128]{4,3,2,1,0:T(8,128)(2,1)} %param.11, s32[]{:T(128)S(6)} %select_n.535, pred[16]{0:T(512)(128)(4,1)S(1)} %iota_compare_fusion.6), kind=kOutput, calls=%fused_computation.71 | convolution fusion | flops 270532608 | bytes 5767684 | tf_op jit(solution)/shard_map/yvg,ygt->yvt/dot_general | solution.py:25
  63.0 5.2 %scatter_fusion.2 = f32[32,128,256]{2,1,0:T(8,128)} fusion(f32[32,128,256]{2,1,0:T(8,128)} %add.522, s32[16]{0:T(128)S(1)} %bitcast.295, f32[16,128,256]{2,1,0:T(8,128)} %fusion.34), kind=kCustom, calls=%fused_computation.20 | custom fusion | flops 524288 | bytes 6291520 | tf_op jit(solution)/shard_map/scatter-add | solution.py:31
  68.3 0.6 gather_fusion.7
  68.9 1.6 collective-permute-start.3
  70.4 3.4 %fusion.33 = f32[16,128,256]{2,1,0:T(8,128)} fusion(bf16[16,128,256]{2,1,0:T(8,128)(2,1)S(1)} %gather_fusion.7, bf16[16,128,256]{2,1,0:T(8,128)(2,1)} %gather_fusion.6, bf16[1,8,16,128,128]{4,3,2,1,0:T(8,128)(2,1)} %param.11, s32[]{:T(128)S(6)} %select_n.542, pred[16]{0:T(512)(128)(4,1)S(1)} %iota_compare_fusion.5), kind=kOutput, calls=%fused_computation.70 | convolution fusion | flops 270532608 | bytes 5767684 | tf_op jit(solution)/shard_map/yvg,ygt->yvt/dot_general | solution.py:25
  73.8 2.5 broadcast.1283.clone.2
  76.3 5.4 %scatter_fusion.3 = f32[32,128,256]{2,1,0:T(8,128)} fusion(f32[32,128,256]{2,1,0:T(8,128)} %broadcast.1283.clone.2, s32[16]{0:T(128)S(1)} %bitcast.294, f32[16,128,256]{2,1,0:T(8,128)} %fusion.33), kind=kCustom, calls=%fused_computation.21 | custom fusion | flops 524288 | bytes 6291520 | tf_op jit(solution)/shard_map/scatter-add | solution.py:31
  81.7 6.2 %add.533 = f32[32,128,256]{2,1,0:T(8,128)} add(f32[32,128,256]{2,1,0:T(8,128)} %scatter_fusion.2, f32[32,128,256]{2,1,0:T(8,128)} %scatter_fusion.3) | non-fusion elementwise | flops 1048576 | bytes 12582912 | tf_op jit(solution)/shard_map/add | solution.py:68
  87.8 1.6 gather_fusion.9
  89.4 1.1 collective-permute-start.4
  90.5 3.4 %fusion.32 = f32[16,128,256]{2,1,0:T(8,128)} fusion(bf16[16,128,256]{2,1,0:T(8,128)(2,1)S(1)} %gather_fusion.9, bf16[16,128,256]{2,1,0:T(8,128)(2,1)} %gather_fusion.8, bf16[1,8,16,128,128]{4,3,2,1,0:T(8,128)(2,1)} %param.11, s32[]{:T(128)S(6)} %select_n.549, pred[16]{0:T(512)(128)(4,1)S(1)} %iota_compare_fusion.4), kind=kOutput, calls=%fused_computation.69 | convolution fusion | flops 270532608 | bytes 5767684 | tf_op jit(solution)/shard_map/yvg,ygt->yvt/dot_general | solution.py:25
  93.9 5.2 %scatter_fusion.4 = f32[32,128,256]{2,1,0:T(8,128)} fusion(f32[32,128,256]{2,1,0:T(8,128)} %add.533, s32[16]{0:T(128)S(1)} %bitcast.293, f32[16,128,256]{2,1,0:T(8,128)} %fusion.32), kind=kCustom, calls=%fused_computation.22 | custom fusion | flops 524288 | bytes 6291520 | tf_op jit(solution)/shard_map/scatter-add | solution.py:31
  99.2 0.6 gather_fusion.11
  99.8 1.9 collective-permute-start.5
  101.7 3.4 %fusion.31 = f32[16,128,256]{2,1,0:T(8,128)} fusion(bf16[16,128,256]{2,1,0:T(8,128)(2,1)S(1)} %gather_fusion.11, bf16[16,128,256]{2,1,0:T(8,128)(2,1)} %gather_fusion.10, bf16[1,8,16,128,128]{4,3,2,1,0:T(8,128)(2,1)} %param.11, s32[]{:T(128)S(6)} %select_n.556, pred[16]{0:T(512)(128)(4,1)S(1)} %iota_compare_fusion.3), kind=kOutput, calls=%fused_computation.68 | convolution fusion | flops 270532608 | bytes 5767684 | tf_op jit(solution)/shard_map/yvg,ygt->yvt/dot_general | solution.py:25
  105.1 2.5 broadcast.1283.clone.3
  107.6 5.2 %scatter_fusion.5 = f32[32,128,256]{2,1,0:T(8,128)} fusion(f32[32,128,256]{2,1,0:T(8,128)} %broadcast.1283.clone.3, s32[16]{0:T(128)S(1)} %bitcast.292, f32[16,128,256]{2,1,0:T(8,128)} %fusion.31), kind=kCustom, calls=%fused_computation.23 | custom fusion | flops 524288 | bytes 6291520 | tf_op jit(solution)/shard_map/scatter-add | solution.py:31
  112.8 6.1 %add.544 = f32[32,128,256]{2,1,0:T(8,128)} add(f32[32,128,256]{2,1,0:T(8,128)} %scatter_fusion.4, f32[32,128,256]{2,1,0:T(8,128)} %scatter_fusion.5) | non-fusion elementwise | flops 1048576 | bytes 12582912 | tf_op jit(solution)/shard_map/add | solution.py:68
  118.9 1.6 gather_fusion.13
  120.9 3.4 %fusion.30 = f32[16,128,256]{2,1,0:T(8,128)} fusion(bf16[16,128,256]{2,1,0:T(8,128)(2,1)S(1)} %gather_fusion.13, bf16[16,128,256]{2,1,0:T(8,128)(2,1)} %gather_fusion.12, bf16[1,8,16,128,128]{4,3,2,1,0:T(8,128)(2,1)} %param.11, s32[]{:T(128)S(6)} %select_n.563, pred[16]{0:T(512)(128)(4,1)S(1)} %iota_compare_fusion.2), kind=kOutput, calls=%fused_computation.67 | convolution fusion | flops 270532608 | bytes 5767684 | tf_op jit(solution)/shard_map/yvg,ygt->yvt/dot_general | solution.py:25
  124.3 5.3 %scatter_fusion.6 = f32[32,128,256]{2,1,0:T(8,128)} fusion(f32[32,128,256]{2,1,0:T(8,128)} %add.544, s32[16]{0:T(128)S(1)} %bitcast.291, f32[16,128,256]{2,1,0:T(8,128)} %fusion.30), kind=kCustom, calls=%fused_computation.24 | custom fusion | flops 524288 | bytes 6291520 | tf_op jit(solution)/shard_map/scatter-add | solution.py:31
  129.6 0.6 gather_fusion.15
  130.2 3.4 %fusion.29 = f32[16,128,256]{2,1,0:T(8,128)} fusion(bf16[16,128,256]{2,1,0:T(8,128)(2,1)S(1)} %gather_fusion.15, bf16[16,128,256]{2,1,0:T(8,128)(2,1)} %gather_fusion.14, bf16[1,8,16,128,128]{4,3,2,1,0:T(8,128)(2,1)} %param.11, s32[]{:T(128)S(6)} %select_n.570, pred[16]{0:T(512)(128)(4,1)S(1)} %iota_compare_fusion.1), kind=kOutput, calls=%fused_computation.66 | convolution fusion | flops 270532608 | bytes 5767684 | tf_op jit(solution)/shard_map/yvg,ygt->yvt/dot_general | solution.py:25
  133.7 2.5 broadcast.1283.clone.4
  136.1 5.2 %scatter_fusion.7 = f32[32,128,256]{2,1,0:T(8,128)} fusion(f32[32,128,256]{2,1,0:T(8,128)} %broadcast.1283.clone.4, s32[16]{0:T(128)S(1)} %bitcast.290, f32[16,128,256]{2,1,0:T(8,128)} %fusion.29), kind=kCustom, calls=%fused_computation.25 | custom fusion | flops 524288 | bytes 6291520 | tf_op jit(solution)/shard_map/scatter-add | solution.py:31
  141.4 4.1 %add.555 = f32[32,128,256]{2,1,0:T(8,128)S(1)} add(f32[32,128,256]{2,1,0:T(8,128)} %scatter_fusion.6, f32[32,128,256]{2,1,0:T(8,128)} %scatter_fusion.7) | non-fusion elementwise | flops 1048576 | bytes 12582912 | tf_op jit(solution)/shard_map/add | solution.py:68
  145.5 2.4 fusion.4
  147.8 13.1 %all-to-all-start = ((bf16[32,128,256]{2,1,0:T(8,128)(2,1)}), bf16[32,128,256]{2,1,0:T(8,128)(2,1)S(1)}, u32[]{:S(2)}, u32[]{:S(2)}) async-start(bf16[32,128,256]{2,1,0:T(8,128)(2,1)} %bitcast.285), calls=%async_computation | async-start | bytes 4194304 | tf_op jit(solution)/shard_map/all_to_all | solution.py:73
  161.0 6.5 %gather_fusion.16 = bf16[128,128,256]{2,1,0:T(8,128)(2,1)} fusion(bf16[4,128,256]{2,1,0:T(8,128)(2,1)S(1)} %bitcast.276, s32[1024]{0:T(1024)S(1)} %get-tuple-element.59), kind=kCustom, calls=%fused_computation.16 | custom fusion | bytes 16777728 | tf_op jit(solution)/shard_map/gather | solution.py:81
  168.1 41.4 %all-to-all-done = bf16[32,128,256]{2,1,0:T(8,128)(2,1)S(1)} async-done(((bf16[32,128,256]{2,1,0:T(8,128)(2,1)}), bf16[32,128,256]{2,1,0:T(8,128)(2,1)S(1)}, u32[]{:S(2)}, u32[]{:S(2)}) %all-to-all-start) | async-done | bytes 2097184 | tf_op jit(solution)/shard_map/all_to_all | solution.py:73
  209.5 6.6 %gather_fusion.17 = bf16[128,128,256]{2,1,0:T(8,128)(2,1)} fusion(bf16[32,128,256]{2,1,0:T(8,128)(2,1)S(1)} %all-to-all-done, s32[1024]{0:T(1024)S(1)} %get-tuple-element.58), kind=kCustom, calls=%fused_computation.17 | custom fusion | bytes 16777728 | tf_op jit(solution)/shard_map/gather | solution.py:81
  216.1 18.5 %fusion.5 = f32[128,128,256]{2,1,0:T(8,128)} fusion(bf16[128,128,256]{2,1,0:T(8,128)(2,1)} %gather_fusion.17, bf16[1,128,128,128]{3,2,1,0:T(8,128)(2,1)} %param.14, pred[128]{0:T(512)(128)(4,1)S(1)} %iota_compare_fusion, bf16[128,128,256]{2,1,0:T(8,128)(2,1)} %gather_fusion.16), kind=kOutput, calls=%fused_computation.36 | convolution fusion | flops 2164260864 | bytes 37748864 | tf_op jit(solution)/shard_map/yvg,ygt->yvt/dot_general | solution.py:25
  234.7 24.1 %scatter_fusion.8 = f32[4,128,256]{2,1,0:T(8,128)S(1)} fusion(f32[4,128,256]{2,1,0:T(8,128)S(1)} %broadcast_in_dim.17, s32[128]{0:T(128)S(1)} %bitcast.298, f32[128,128,256]{2,1,0:T(8,128)} %fusion.5), kind=kCustom, calls=%fused_computation.26 | custom fusion | flops 4194304 | bytes 50332160 | tf_op jit(solution)/shard_map/scatter-add | solution.py:31
  258.8 0.8 fusion.55
  (43 shorter events, 1.2 us)
Async XLA Ops:
  0.6 36.8 %collective-permute-start = (bf16[512,256]{1,0:T(8,128)(2,1)}, bf16[512,256]{1,0:T(8,128)(2,1)S(1)}, u32[]{:S(2)}, u32[]{:S(2)}) collective-permute-start(bf16[512,256]{1,0:T(8,128)(2,1)} %param.9), channel_id=1, source_target_pairs={{0,32},{32,64},{64,96},{96,128},{128,160},{160,192},{192,224},{224... | collective-permute-start | bytes 786440 | tf_op jit(solution)/shard_map/ppermute | solution.py:14
  11.0 7.4 %copy-start.1 = (bf16[4096,256]{1,0:T(8,128)(2,1)S(1)}, bf16[4096,256]{1,0:T(8,128)(2,1)}, u32[]{:S(2)}) copy-start(bf16[4096,256]{1,0:T(8,128)(2,1)} %param.8) | copy-start | bytes 6291460
  38.0 18.6 %collective-permute-start.1 = (bf16[512,256]{1,0:T(8,128)(2,1)S(1)}, bf16[512,256]{1,0:T(8,128)(2,1)}, u32[]{:S(2)}, u32[]{:S(2)}) collective-permute-start(bf16[512,256]{1,0:T(8,128)(2,1)S(1)} %collective-permute-done), channel_id=1, source_target_pairs={{0,32},{32,64},{64,96},{96,128},{128,160},{160,192},{192,224},{224... | collective-permute-start | bytes 786440 | tf_op jit(solution)/shard_map/ppermute | solution.py:14
  58.2 10.1 %collective-permute-start.2 = (bf16[512,256]{1,0:T(8,128)(2,1)}, bf16[512,256]{1,0:T(8,128)(2,1)S(1)}, u32[]{:S(2)}, u32[]{:S(2)}) collective-permute-start(bf16[512,256]{1,0:T(8,128)(2,1)} %collective-permute-done.1), channel_id=1, source_target_pairs={{0,32},{32,64},{64,96},{96,128},{128,160},{160,192},{192,224},{224... | collective-permute-start | bytes 786440 | tf_op jit(solution)/shard_map/ppermute | solution.py:14
  68.9 18.9 %collective-permute-start.3 = (bf16[512,256]{1,0:T(8,128)(2,1)S(1)}, bf16[512,256]{1,0:T(8,128)(2,1)}, u32[]{:S(2)}, u32[]{:S(2)}) collective-permute-start(bf16[512,256]{1,0:T(8,128)(2,1)S(1)} %collective-permute-done.2), channel_id=1, source_target_pairs={{0,32},{32,64},{64,96},{96,128},{128,160},{160,192},{192,224},{224... | collective-permute-start | bytes 786440 | tf_op jit(solution)/shard_map/ppermute | solution.py:14
  89.4 9.8 %collective-permute-start.4 = (bf16[512,256]{1,0:T(8,128)(2,1)}, bf16[512,256]{1,0:T(8,128)(2,1)S(1)}, u32[]{:S(2)}, u32[]{:S(2)}) collective-permute-start(bf16[512,256]{1,0:T(8,128)(2,1)} %collective-permute-done.3), channel_id=1, source_target_pairs={{0,32},{32,64},{64,96},{96,128},{128,160},{160,192},{192,224},{224... | collective-permute-start | bytes 786440 | tf_op jit(solution)/shard_map/ppermute | solution.py:14
  99.8 19.1 %collective-permute-start.5 = (bf16[512,256]{1,0:T(8,128)(2,1)S(1)}, bf16[512,256]{1,0:T(8,128)(2,1)}, u32[]{:S(2)}, u32[]{:S(2)}) collective-permute-start(bf16[512,256]{1,0:T(8,128)(2,1)S(1)} %collective-permute-done.4), channel_id=1, source_target_pairs={{0,32},{32,64},{64,96},{96,128},{128,160},{160,192},{192,224},{224... | collective-permute-start | bytes 786440 | tf_op jit(solution)/shard_map/ppermute | solution.py:14
  120.5 9.1 %collective-permute-start.6 = (bf16[512,256]{1,0:T(8,128)(2,1)}, bf16[512,256]{1,0:T(8,128)(2,1)S(1)}, u32[]{:S(2)}, u32[]{:S(2)}) collective-permute-start(bf16[512,256]{1,0:T(8,128)(2,1)} %collective-permute-done.5), channel_id=1, source_target_pairs={{0,32},{32,64},{64,96},{96,128},{128,160},{160,192},{192,224},{224... | collective-permute-start | bytes 786440 | tf_op jit(solution)/shard_map/ppermute | solution.py:14
  147.8 13.1 %copy-start.2 = (s32[1,128]{1,0:T(1,128)S(1)}, s32[1,128]{1,0:T(1,128)}, u32[]{:S(2)}) copy-start(s32[1,128]{1,0:T(1,128)} %param.13) | copy-start | bytes 1540
  147.8 13.1 %copy-start = (bf16[512,256]{1,0:T(8,128)(2,1)S(1)}, bf16[512,256]{1,0:T(8,128)(2,1)}, u32[]{:S(2)}) copy-start(bf16[512,256]{1,0:T(8,128)(2,1)} %param.9) | copy-start | bytes 786436
  147.8 61.7 %all-to-all-start = ((bf16[32,128,256]{2,1,0:T(8,128)(2,1)}), bf16[32,128,256]{2,1,0:T(8,128)(2,1)S(1)}, u32[]{:S(2)}, u32[]{:S(2)}) async-start(bf16[32,128,256]{2,1,0:T(8,128)(2,1)} %bitcast.285), calls=%async_computation | async-start | bytes 4194304 | tf_op jit(solution)/shard_map/all_to_all | solution.py:73
where the time goes:
time: 264 us; the launch traced here: 260 us
  other arithmetic  98.1 us (37%)
  local copies, waits for them, and re-layouts  50.4 us (19%)
  matrix products  45.7 us (17%)
  waiting for transfers between devices  41.4 us (16%)
  starting transfers between devices  22.2 us (8%)
    scatter-add x9, other arithmetic, collect(): return jax.ops.segment_sum(terms, block_index, num_segments=count_of_blocks)  66.2 us
    dot_general x9, matrix products, block_loss_terms(): jnp.einsum('yvg,ygt->yvt', rating_error, column_factor_matrix, preferred_...  45.7 us
    all_to_all x1, waiting for transfers between devices, per_device(): lax.all_to_all(new_users, 'wide', split_axis=0, concat_axis=0, tiled=True)  41.4 us
    add x4, other arithmetic, per_device(): user_total + collect(visit_terms, visit_user_index, user_blocks)  22.5 us
    gather x8, local copies, waits for them, and re-layouts, per_device(): row_factor_matrix = own_users[visit_user_index]  14.6 us
    all_to_all x1, starting transfers between devices, per_device(): lax.all_to_all(new_users, 'wide', split_axis=0, concat_axis=0, tiled=True)  13.1 us
    another operation x5, local copies, waits for them, and re-layouts  12.3 us
    ppermute x7, starting transfers between devices, from_behind(): return lax.ppermute(value, axis, pairs)  9.09 us
  transfers between devices with their start and end apart: 8, of which 1 were waited for; matrix products, arithmetic and copies ran while one was open for 46% of the time, Pallas kernels for 0%

commit v1 on v0

v1 whole, which is shorter than its diff:
```python
import jax
import jax.numpy as jnp
from jax import lax
from jax.experimental import pallas as pl
from jax.experimental.pallas import tpu as pltpu
from jax.sharding import PartitionSpec as P

MESH = pl.DeviceIdType.MESH

user_rate = 0.03
item_rate = 0.005
shrink = 0.05

B = 128
R = 256
UB = 32
IB = 4
NS = 8
CAP = 16
NSLOT = NS * CAP

ORDER = ((0, 0), (0, 1), (0, 3), (1, 0), (0, 2), (1, 1), (1, 3), (1, 2))


def nt(a, b):
    return lax.dot_general(a, b, (((1,), (1,)), ((), ())), preferred_element_type=jnp.float32)


def nn(a, b):
    return lax.dot_general(a, b, (((1,), (0,)), ((), ())), preferred_element_type=jnp.float32)


def kernel(
    users, items, pairs, ratings, counts, ipairs, iratings, icount,
    new_users, new_items,
    h00, h01, h02, h03, h10, h11, h12, h13,
    users_v, ur_v, ir_v, terms, nu_v, recv, acc, ni_v,
    pairs_s, counts_s, icount_s, pairs_v, ipairs_v, tab_v, tab_s,
    lsem, ursem, gs, gr, ss, rs, osem,
):
    blk = lax.axis_index("blk")
    wide = lax.axis_index("wide")
    xh, y = lax.div(blk, 4), lax.rem(blk, 4)
    xl, z, core = lax.div(wide, 16), lax.rem(lax.div(wide, 2), 8), lax.rem(wide, 2)
    held = {(0, 0): h00, (0, 1): h01, (0, 2): h02, (0, 3): h03,
            (1, 0): h10, (1, 1): h11, (1, 2): h12, (1, 3): h13}

    def slice_of(fx, dy):
        return lax.rem(xh + fx, 2) * 4 + lax.rem(y + 4 - dy, 4)

    up = (xh * 4 + lax.rem(y + 1, 4), wide)
    down = (xh * 4 + lax.rem(y + 3, 4), wide)
    across = (lax.rem(blk + 4, 8), wide)

    def partner(t, sign):
        d = lax.div(t, 4)
        dz = jnp.where(lax.rem(d, 2) == 0, lax.div(d, 2) + 1, 8 - 1 - lax.div(d, 2))
        dz = jnp.where(t >= 28, 0, dz)
        e = jnp.where(t >= 28, t - 27, lax.rem(t, 4))
        zz = lax.rem(z + 8 + sign * dz, 8)
        xx = lax.rem(xl + lax.div(e, 2), 2)
        cc = lax.rem(core + lax.rem(e, 2), 2)
        return xx * 16 + zz * 2 + cc

    barrier = pltpu.get_barrier_semaphore()
    for dev in (up, down, across):
        pl.semaphore_signal(barrier, inc=1, device_id=dev, device_id_type=MESH)

    def greet(t, carry):
        pl.semaphore_signal(barrier, inc=1, device_id=(blk, partner(t, 1)), device_id_type=MESH)
        return carry

    lax.fori_loop(0, UB - 1, greet, 0)

    local = [
        pltpu.make_async_copy(items, h00.reshape(IB * B, R), lsem.at[0]),
        pltpu.make_async_copy(pairs, pairs_v, lsem.at[1]),
        pltpu.make_async_copy(ipairs, ipairs_v, lsem.at[2]),
        pltpu.make_async_copy(pairs, pairs_s, lsem.at[3]),
        pltpu.make_async_copy(counts, counts_s, lsem.at[4]),
        pltpu.make_async_copy(icount, icount_s, lsem.at[5]),
        pltpu.make_async_copy(users, users_v.reshape(UB * B, R), lsem.at[6]),
    ]
    for copy in local:
        copy.start()
    rating_copies = []
    for j, (fx, dy) in enumerate(ORDER):
        copy = pltpu.make_async_copy(ratings.at[0, slice_of(fx, dy)], ur_v.at[j], ursem.at[j])
        copy.start()
        rating_copies.append(copy)
    irating_copy = pltpu.make_async_copy(iratings.at[0], ir_v.at[pl.ds(0, NSLOT)], lsem.at[7])
    irating_copy.start()

    pl.semaphore_wait(barrier, 3 + UB - 1)

    def send(n, src, dst, dev):
        return pltpu.make_async_remote_copy(
            src_ref=src, dst_ref=dst, send_sem=gs.at[n], recv_sem=gr.at[n], device_id=dev, device_id_type=MESH
        )

    lo, hi = pl.ds(0, IB // 2), pl.ds(IB // 2, IB // 2)
    local[0].wait()
    hops = {}

    def go(n, src, dst, dev):
        hops[n] = send(n, src, dst, dev)
        hops[n].start()

    go(0, h00, h01, up)
    go(1, h00, h03, down)
    go(2, h00, h10, across)

    terms[NSLOT] = jnp.zeros((B, R), jnp.float32)
    ir_v[NSLOT] = jnp.zeros((B, B), jnp.bfloat16)
    for n in (1, 2, 5):
        local[n].wait()
    sub = lax.broadcasted_iota(jnp.int32, (B, B), 0)
    lane = lax.broadcasted_iota(jnp.int32, (B, B), 1)
    k16 = lax.broadcasted_iota(jnp.int32, (CAP, B), 0)
    l16 = lax.broadcasted_iota(jnp.int32, (CAP, B), 1)
    spread = jnp.where(lax.rem(l16, CAP) == k16, jnp.float32(1), jnp.float32(0)).astype(jnp.bfloat16)
    wide_pairs = nn(pairs_v[0].astype(jnp.float32).astype(jnp.bfloat16), spread)
    s8 = lax.broadcasted_iota(jnp.int32, (NS, B), 0)
    j8 = lax.div(lax.broadcasted_iota(jnp.int32, (NS, B), 1), CAP)
    picked = jnp.zeros((NS, B), jnp.bool_)
    for j, (fx, dy) in enumerate(ORDER):
        picked = picked | ((j8 == j) & (s8 == slice_of(fx, dy)))
    pair_row = jnp.sum(jnp.where(picked, wide_pairs, 0.0), axis=0, keepdims=True)
    user_row = jnp.floor(pair_row * 0.25)
    user_here = jnp.broadcast_to(user_row, (B, B))
    user_there = user_here.T
    before = jnp.max(jnp.where((user_here == user_there) & (sub < lane), sub, -1), axis=0, keepdims=True)
    last = jnp.max(jnp.where(user_there == lane.astype(jnp.float32), sub, -1), axis=0, keepdims=True)
    item_row = jnp.broadcast_to(ipairs_v[...].astype(jnp.float32), (B, B)).T
    slot_of = jnp.min(
        jnp.where((item_row == lane.astype(jnp.float32)) & (sub < icount_s[0]), sub, NSLOT), axis=0, keepdims=True
    )
    tab_v[0:1, :] = jnp.where(before < 0, NSLOT, before)
    tab_v[1:2, :] = jnp.where(last < 0, NSLOT, last)
    tab_v[2:3, :] = slot_of
    tab_copy = pltpu.make_async_copy(tab_v, tab_s, lsem.at[8])
    tab_copy.start()
    for n in (3, 4, 6):
        local[n].wait()
    tab_copy.wait()

    STEP = 4

    def work(j):
        fx, dy = ORDER[j]
        cols_ref = held[(fx, dy)]
        s = slice_of(fx, dy)
        rating_copies[j].wait()
        live = counts_s[0, s]

        def body(g, carry):
            cols, errs = [], []
            for e in range(STEP):
                k = g * STEP + e
                p = pairs_s[0, s, k]
                rows = users_v[lax.shift_right_logical(p, 2)]
                col = cols_ref[lax.bitwise_and(p, 3)]
                r = ur_v[j, k].astype(jnp.float32)
                seen = (r != 0) & (k < live)
                errs.append(jnp.where(seen, r - nt(rows, col), 0.0).astype(jnp.bfloat16))
                cols.append(col)
            for e in range(STEP):
                n = j * CAP + g * STEP + e
                terms[n] = terms[tab_s[0, n]] + nn(errs[e], cols[e])
            return carry

        lax.fori_loop(0, CAP // STEP, body, 0)

    work(0)
    hops[0].wait_recv()
    go(3, h01.at[lo], h02.at[lo], up)
    hops[1].wait_recv()
    go(4, h03.at[hi], h02.at[hi], down)
    hops[2].wait_recv()
    go(5, h10, h11, up)
    go(6, h10, h13, down)
    work(1)
    work(2)
    work(3)
    hops[3].wait_recv()
    hops[4].wait_recv()
    work(4)
    hops[5].wait_recv()
    go(7, h11.at[lo], h12.at[lo], up)
    hops[6].wait_recv()
    go(8, h13.at[hi], h12.at[hi], down)
    work(5)
    work(6)
    hops[7].wait_recv()
    hops[8].wait_recv()
    work(7)

    def update(u):
        old = users_v[u].astype(jnp.float32)
        total = terms[tab_s[1, u]]
        nu_v[u] = (old + user_rate * (total - shrink * old)).astype(jnp.bfloat16)

    def relay(t):
        u = partner(t, 1)
        return pltpu.make_async_remote_copy(
            src_ref=nu_v.at[u], dst_ref=recv.at[t], send_sem=ss.at[t], recv_sem=rs.at[t],
            device_id=(blk, u), device_id_type=MESH,
        )

    def send_out(t, carry):
        update(partner(t, 1))
        relay(t).start()
        return carry

    lax.fori_loop(0, UB - 1, send_out, 0)
    update(wide)
    recv[UB - 1] = nu_v[wide]
    users_out = pltpu.make_async_copy(nu_v.reshape(UB * B, R), new_users, osem.at[0])
    users_out.start()
    irating_copy.wait()
    acc[...] = jnp.zeros_like(acc)

    def absorb(first, second, t):
        both = recv[pl.ds(t, 2)].reshape(2 * B, R)
        for i in range(IB):
            rate = jnp.concatenate(
                [ir_v[tab_s[2, i * UB + first]], ir_v[tab_s[2, i * UB + second]]], axis=1
            ).astype(jnp.float32)
            err = jnp.where(rate != 0, rate - nt(h00[i], both), 0.0).astype(jnp.bfloat16)
            acc[i] += nn(err, both)

    def take(q, carry):
        t = q * 2
        relay(t).wait_recv()
        relay(t + 1).wait_recv()
        absorb(partner(t, -1), partner(t + 1, -1), t)
        return carry

    lax.fori_loop(0, UB // 2 - 1, take, 0)
    relay(UB - 2).wait_recv()
    absorb(partner(UB - 2, -1), wide, UB - 2)
    old = h00[...].astype(jnp.float32)
    ni_v[...] = (old + item_rate * (acc[...] - shrink * old)).astype(jnp.bfloat16)
    items_out = pltpu.make_async_copy(ni_v.reshape(IB * B, R), new_items, osem.at[1])
    items_out.start()

    for n in hops:
        hops[n].wait_send()

    def sent(t, carry):
        relay(t).wait_send()
        return carry

    lax.fori_loop(0, UB - 1, sent, 0)
    users_out.wait()
    items_out.wait()


def per_device(
    users, items, user_pairs, user_ratings, user_counts, item_pairs, item_ratings, live_item_counts
):
    bf, f32, i32 = jnp.bfloat16, jnp.float32, jnp.int32
    return pl.pallas_call(
        kernel,
        out_shape=(
            jax.ShapeDtypeStruct(users.shape, bf),
            jax.ShapeDtypeStruct(items.shape, bf),
        ),
        in_specs=[pl.BlockSpec(memory_space=pl.ANY)] * 8,
        out_specs=(pl.BlockSpec(memory_space=pl.ANY), pl.BlockSpec(memory_space=pl.ANY)),
        scratch_shapes=[pltpu.VMEM((IB, B, R), bf)] * 8
        + [
            pltpu.VMEM((UB, B, R), bf),
            pltpu.VMEM((NS, CAP, B, B), bf),
            pltpu.VMEM((NSLOT + 1, B, B), bf),
            pltpu.VMEM((NSLOT + 1, B, R), f32),
            pltpu.VMEM((UB, B, R), bf),
            pltpu.VMEM((UB, B, R), bf),
            pltpu.VMEM((IB, B, R), f32),
            pltpu.VMEM((IB, B, R), bf),
            pltpu.SMEM((1, NS, CAP), i32),
            pltpu.SMEM((1, NS), i32),
            pltpu.SMEM((1,), i32),
            pltpu.VMEM((1, NS, CAP), i32),
            pltpu.VMEM((1, NSLOT), i32),
            pltpu.VMEM((8, 128), i32),
            pltpu.SMEM((8, 128), i32),
            pltpu.SemaphoreType.DMA((9,)),
            pltpu.SemaphoreType.DMA((NS,)),
            pltpu.SemaphoreType.DMA((9,)),
            pltpu.SemaphoreType.DMA((9,)),
            pltpu.SemaphoreType.DMA((UB - 1,)),
            pltpu.SemaphoreType.DMA((UB - 1,)),
            pltpu.SemaphoreType.DMA((2,)),
        ],
        compiler_params=pltpu.CompilerParams(
            collective_id=0, has_side_effects=True, vmem_limit_bytes=52 * 2**20
        ),
        name="round",
    )(users, items, user_pairs, user_ratings, user_counts, item_pairs, item_ratings, live_item_counts)


def solution(mesh):
    return jax.shard_map(
        per_device,
        mesh=mesh,
        in_specs=(
            P(("blk", "wide"), None),
            P(("blk", "wide"), None),
            P(("blk", "wide"), None, None),
            P(("blk", "wide"), None, None, None, None),
            P(("blk", "wide"), None),
            P(("blk", "wide"), None),
            P(("blk", "wide"), None, None, None),
            P(("blk", "wide")),
        ),
        out_specs=(P(("blk", "wide"), None), P(("blk", "wide"), None)),
        check_vma=False,
    )
```

time: 264 us -> 93.2 us (0.35)
  the two profiles are of different devices: /device:TPU:11 before, /device:TPU:69 now
where the time goes in v1:
time: 93.2 us; the launch traced here: 93 us
  Pallas kernels  85 us (91%)
  local copies, waits for them, and re-layouts  6.69 us (7%)
  between operations  1.3 us (1%)
    pallas_call x1, Pallas kernels, per_device(): pl.pallas_call(kernel, out_shape=(jax.ShapeDtypeStruct(users.shape, bf),...  85 us
    unnamed x10, local copies, waits for them, and re-layouts  6.69 us

profile of v1, /device:TPU:69, one launch (start us, length us, event | category | flops | bytes accessed | tf_op | source)
XLA Modules:
  0.0 93.0 jit_solution(3041061911300553791)
XLA Ops:
  1.3 0.0 copy-start
  1.3 0.9 %copy-done = bf16[512,256]{1,0:T(8,128)(2,1)S(1)} copy-done((bf16[512,256]{1,0:T(8,128)(2,1)S(1)}, bf16[512,256]{1,0:T(8,128)(2,1)}, u32[]{:S(2)}) %copy-start) | copy-done | bytes 262168
  2.2 0.0 copy-start.1
  2.2 0.7 copy-done.1
  2.9 0.0 copy-start.2
  2.9 0.7 copy-done.2
  3.6 0.0 copy-start.3
  3.6 0.7 copy-done.3
  4.2 85.0 %round.1 = (bf16[4096,256]{1,0:T(8,128)(2,1)}, bf16[512,256]{1,0:T(8,128)(2,1)S(1)}) custom-call(bf16[4096,256]{1,0:T(8,128)(2,1)} %users.1, bf16[512,256]{1,0:T(8,128)(2,1)S(1)} %copy-done, s32[1,8,16]{2,1,0:T(8,128)S(1)} %copy-done.1, bf16[1,8,16,128,128]{4,3,2,1,0:T(8,128)(2,1)} %ratings.1, s32[1,8]{1,0:T(1,128)S(1)} %copy-done.2, ...), custom_call_target="tpu_custom_call" | custom-call | tf_op jit(solution)/shard_map/round/pallas_call | solution.py:263
  89.2 3.0 %copy.13 = bf16[4096,256]{1,0:T(8,128)(2,1)} copy(bf16[4096,256]{1,0:T(8,128)(2,1)} %get-tuple-element.4) | data formatting | bytes 4194304
  92.3 0.7 copy.14
Async XLA Ops:
  1.3 1.0 %copy-start = (bf16[512,256]{1,0:T(8,128)(2,1)S(1)}, bf16[512,256]{1,0:T(8,128)(2,1)}, u32[]{:S(2)}) copy-start(bf16[512,256]{1,0:T(8,128)(2,1)} %items.1) | copy-start | bytes 786436
  2.2 0.7 copy-start.1
  2.9 0.7 copy-start.2
  3.6 0.7 copy-start.3

commit v2 on v1

--- a/solution.py
+++ b/solution.py
@@ -18,6 +18,8 @@
 NS = 8
 CAP = 16
 NSLOT = NS * CAP
+VMEM = 62 * 2**20
+PIECES = 4
 
 ORDER = ((0, 0), (0, 1), (0, 3), (1, 0), (0, 2), (1, 1), (1, 3), (1, 2))
 
@@ -36,7 +38,7 @@
     h00, h01, h02, h03, h10, h11, h12, h13,
     users_v, ur_v, ir_v, terms, nu_v, recv, acc, ni_v,
     pairs_s, counts_s, icount_s, pairs_v, ipairs_v, tab_v, tab_s,
-    lsem, ursem, gs, gr, ss, rs, osem,
+    lsem, ursem, gs, gr, ss, rs, osem, token, entered,
 ):
     blk = lax.axis_index("blk")
     wide = lax.axis_index("wide")
@@ -62,24 +64,32 @@
         cc = lax.rem(core + lax.rem(e, 2), 2)
         return xx * 16 + zz * 2 + cc
 
+    place = z
+    below = xl * 16 + lax.rem(z + 7, 8) * 2 + core
+    above = xl * 16 + lax.rem(z + 1, 8) * 2 + core
+    plane = (
+        xl * 16 + z * 2 + 1 - core,
+        (1 - xl) * 16 + z * 2 + core,
+        (1 - xl) * 16 + z * 2 + 1 - core,
+    )
     barrier = pltpu.get_barrier_semaphore()
     for dev in (up, down, across):
         pl.semaphore_signal(barrier, inc=1, device_id=dev, device_id_type=MESH)
-
-    def greet(t, carry):
-        pl.semaphore_signal(barrier, inc=1, device_id=(blk, partner(t, 1)), device_id_type=MESH)
-        return carry
-
-    lax.fori_loop(0, UB - 1, greet, 0)
+    for dev in plane:
+        pl.semaphore_signal(barrier, inc=1, device_id=(blk, dev), device_id_type=MESH)
+
+    @pl.when(place > 0)
+    def _():
+        pl.semaphore_signal(barrier, inc=1, device_id=(blk, below), device_id_type=MESH)
 
     local = [
-        pltpu.make_async_copy(items, h00.reshape(IB * B, R), lsem.at[0]),
+        pltpu.make_async_copy(items, h00, lsem.at[0]),
         pltpu.make_async_copy(pairs, pairs_v, lsem.at[1]),
         pltpu.make_async_copy(ipairs, ipairs_v, lsem.at[2]),
         pltpu.make_async_copy(pairs, pairs_s, lsem.at[3]),
         pltpu.make_async_copy(counts, counts_s, lsem.at[4]),
         pltpu.make_async_copy(icount, icount_s, lsem.at[5]),
-        pltpu.make_async_copy(users, users_v.reshape(UB * B, R), lsem.at[6]),
+        pltpu.make_async_copy(users, users_v, lsem.at[6]),
     ]
     for copy in local:
         copy.start()
@@ -91,7 +101,7 @@
     irating_copy = pltpu.make_async_copy(iratings.at[0], ir_v.at[pl.ds(0, NSLOT)], lsem.at[7])
     irating_copy.start()
 
-    pl.semaphore_wait(barrier, 3 + UB - 1)
+    pl.semaphore_wait(barrier, 6 + jnp.where(place < 7, 1, 0))
 
     def send(n, src, dst, dev):
         return pltpu.make_async_remote_copy(
@@ -99,16 +109,34 @@
         )
 
     lo, hi = pl.ds(0, IB // 2), pl.ds(IB // 2, IB // 2)
-    local[0].wait()
     hops = {}
 
-    def go(n, src, dst, dev):
-        hops[n] = send(n, src, dst, dev)
+    def go(n, src, dst, half, dev):
+        hops[n] = send(n, src.at[half], dst.at[half], dev)
         hops[n].start()
 
-    go(0, h00, h01, up)
-    go(1, h00, h03, down)
-    go(2, h00, h10, across)
+    go(0, items, h01, lo, up)
+    go(1, items, h03, hi, down)
+    go(2, items, h10, lo, across)
+    go(3, items, h10, hi, across)
+    go(4, items, h01, hi, up)
+    go(5, items, h03, lo, down)
+
+    @pl.when(place > 0)
+    def _():
+        pl.semaphore_wait(token, 1)
+
+    @pl.when(place < 7)
+    def _():
+        pl.semaphore_signal(token, inc=1, device_id=(blk, above), device_id_type=MESH)
+
+    def greet(n, carry):
+        e, zz = lax.rem(n, 4), lax.div(n, 4)
+        dev = lax.div(e, 2) * 16 + zz * 2 + lax.rem(e, 2)
+        pl.semaphore_signal(entered, inc=1, device_id=(blk, dev), device_id_type=MESH)
+        return carry
+
+    lax.fori_loop(0, 4 * place, greet, 0)
 
     terms[NSLOT] = jnp.zeros((B, R), jnp.float32)
     ir_v[NSLOT] = jnp.zeros((B, B), jnp.bfloat16)
@@ -144,7 +172,7 @@
         local[n].wait()
     tab_copy.wait()
 
-    STEP = 4
+    STEP = 8
 
     def work(j):
         fx, dy = ORDER[j]
@@ -171,29 +199,41 @@
 
         lax.fori_loop(0, CAP // STEP, body, 0)
 
+    local[0].wait()
     work(0)
     hops[0].wait_recv()
-    go(3, h01.at[lo], h02.at[lo], up)
+    go(6, h01, h02, lo, up)
+    go(7, h01, h11, lo, across)
     hops[1].wait_recv()
-    go(4, h03.at[hi], h02.at[hi], down)
+    go(8, h03, h02, hi, down)
+    go(9, h03, h13, hi, across)
     hops[2].wait_recv()
-    go(5, h10, h11, up)
-    go(6, h10, h13, down)
+    hops[3].wait_recv()
+    go(10, h10, h11, hi, up)
+    go(11, h10, h13, lo, down)
+    hops[4].wait_recv()
     work(1)
+    hops[5].wait_recv()
     work(2)
     work(3)
-    hops[3].wait_recv()
-    hops[4].wait_recv()
+    hops[6].wait_recv()
+    hops[8].wait_recv()
     work(4)
-    hops[5].wait_recv()
-    go(7, h11.at[lo], h12.at[lo], up)
-    hops[6].wait_recv()
-    go(8, h13.at[hi], h12.at[hi], down)
+    hops[7].wait_recv()
+    go(12, h11, h12, lo, up)
+    hops[9].wait_recv()
+    go(13, h13, h12, hi, down)
+    hops[10].wait_recv()
     work(5)
+    hops[11].wait_recv()
     work(6)
-    hops[7].wait_recv()
-    hops[8].wait_recv()
+    hops[12].wait_recv()
+    hops[13].wait_recv()
     work(7)
+
+    @pl.when(place < 7)
+    def _():
+        pl.semaphore_wait(entered, 4 * (7 - place))
 
     def update(u):
         old = users_v[u].astype(jnp.float32)
@@ -215,33 +255,37 @@
     lax.fori_loop(0, UB - 1, send_out, 0)
     update(wide)
     recv[UB - 1] = nu_v[wide]
-    users_out = pltpu.make_async_copy(nu_v.reshape(UB * B, R), new_users, osem.at[0])
+    users_out = pltpu.make_async_copy(nu_v, new_users, osem.at[0])
     users_out.start()
     irating_copy.wait()
     acc[...] = jnp.zeros_like(acc)
 
-    def absorb(first, second, t):
-        both = recv[pl.ds(t, 2)].reshape(2 * B, R)
+    GROUP = 4
+
+    def absorb(t, owners):
+        some = recv[pl.ds(t, GROUP)].reshape(GROUP * B, R)
+        guess = nt(h00[...].reshape(IB * B, R), some)
+        errs = []
         for i in range(IB):
-            rate = jnp.concatenate(
-                [ir_v[tab_s[2, i * UB + first]], ir_v[tab_s[2, i * UB + second]]], axis=1
-            ).astype(jnp.float32)
-            err = jnp.where(rate != 0, rate - nt(h00[i], both), 0.0).astype(jnp.bfloat16)
-            acc[i] += nn(err, both)
+            rate = jnp.concatenate([ir_v[tab_s[2, i * UB + u]] for u in owners], axis=1).astype(jnp.float32)
+            errs.append(jnp.where(rate != 0, rate - guess[i * B : (i + 1) * B], 0.0).astype(jnp.bfloat16))
+        acc[...] += nn(jnp.concatenate(errs, axis=0), some).reshape(IB, B, R)
 
     def take(q, carry):
-        t = q * 2
-        relay(t).wait_recv()
-        relay(t + 1).wait_recv()
-        absorb(partner(t, -1), partner(t + 1, -1), t)
+        t = q * GROUP
+        for e in range(GROUP):
+            relay(t + e).wait_recv()
+        absorb(t, [partner(t + e, -1) for e in range(GROUP)])
         return carry
 
-    lax.fori_loop(0, UB // 2 - 1, take, 0)
-    relay(UB - 2).wait_recv()
-    absorb(partner(UB - 2, -1), wide, UB - 2)
+    lax.fori_loop(0, UB // GROUP - 1, take, 0)
+    t = UB - GROUP
+    for e in range(GROUP - 1):
+        relay(t + e).wait_recv()
+    absorb(t, [partner(t + e, -1) for e in range(GROUP - 1)] + [wide])
     old = h00[...].astype(jnp.float32)
     ni_v[...] = (old + item_rate * (acc[...] - shrink * old)).astype(jnp.bfloat16)
-    items_out = pltpu.make_async_copy(ni_v.reshape(IB * B, R), new_items, osem.at[1])
+    items_out = pltpu.make_async_copy(ni_v, new_items, osem.at[1])
     items_out.start()
 
     for n in hops:
@@ -254,17 +298,33 @@
     lax.fori_loop(0, UB - 1, sent, 0)
     users_out.wait()
     items_out.wait()
+
+
+def deliver(made_users, made_items, new_users, new_items, held_users, held_items, insem, outsem):
+    parts = [(made_items, held_items, new_items)]
+    for n in range(PIECES):
+        part = pl.ds(n * (UB // PIECES), UB // PIECES)
+        parts.append((made_users.at[part], held_users.at[part], new_users.at[part]))
+    reads = [pltpu.make_async_copy(a, b, insem.at[n]) for n, (a, b, c) in enumerate(parts)]
+    writes = [pltpu.make_async_copy(b, c, outsem.at[n]) for n, (a, b, c) in enumerate(parts)]
+    for copy in reads:
+        copy.start()
+    for read, write in zip(reads, writes):
+        read.wait()
+        write.start()
+    for copy in writes:
+        copy.wait()
 
 
 def per_device(
     users, items, user_pairs, user_ratings, user_counts, item_pairs, item_ratings, live_item_counts
 ):
     bf, f32, i32 = jnp.bfloat16, jnp.float32, jnp.int32
-    return pl.pallas_call(
+    made_users, made_items = pl.pallas_call(
         kernel,
         out_shape=(
-            jax.ShapeDtypeStruct(users.shape, bf),
-            jax.ShapeDtypeStruct(items.shape, bf),
+            jax.ShapeDtypeStruct((UB, B, R), bf),
+            jax.ShapeDtypeStruct((IB, B, R), bf),
         ),
         in_specs=[pl.BlockSpec(memory_space=pl.ANY)] * 8,
         out_specs=(pl.BlockSpec(memory_space=pl.ANY), pl.BlockSpec(memory_space=pl.ANY)),
@@ -287,17 +347,40 @@
             pltpu.SMEM((8, 128), i32),
             pltpu.SemaphoreType.DMA((9,)),
             pltpu.SemaphoreType.DMA((NS,)),
-            pltpu.SemaphoreType.DMA((9,)),
-            pltpu.SemaphoreType.DMA((9,)),
+            pltpu.SemaphoreType.DMA((14,)),
+            pltpu.SemaphoreType.DMA((14,)),
             pltpu.SemaphoreType.DMA((UB - 1,)),
             pltpu.SemaphoreType.DMA((UB - 1,)),
             pltpu.SemaphoreType.DMA((2,)),
+            pltpu.SemaphoreType.REGULAR,
+            pltpu.SemaphoreType.REGULAR,
         ],
         compiler_params=pltpu.CompilerParams(
-            collective_id=0, has_side_effects=True, vmem_limit_bytes=52 * 2**20
+            collective_id=0, has_side_effects=True, vmem_limit_bytes=VMEM
         ),
         name="round",
-    )(users, items, user_pairs, user_ratings, user_counts, item_pairs, item_ratings, live_item_counts)
+    )(
+        users.reshape(UB, B, R), items.reshape(IB, B, R),
+        user_pairs, user_ratings, user_counts, item_pairs, item_ratings, live_item_counts,
+    )
+    new_users, new_items = pl.pallas_call(
+        deliver,
+        out_shape=(
+            jax.ShapeDtypeStruct((UB, B, R), bf),
+            jax.ShapeDtypeStruct((IB, B, R), bf),
+        ),
+        in_specs=[pl.BlockSpec(memory_space=pl.ANY)] * 2,
+        out_specs=(pl.BlockSpec(memory_space=pl.ANY), pl.BlockSpec(memory_space=pl.ANY)),
+        scratch_shapes=[
+            pltpu.VMEM((UB, B, R), bf),
+            pltpu.VMEM((IB, B, R), bf),
+            pltpu.SemaphoreType.DMA((PIECES + 1,)),
+            pltpu.SemaphoreType.DMA((PIECES + 1,)),
+        ],
+        compiler_params=pltpu.CompilerParams(vmem_limit_bytes=VMEM),
+        name="deliver",
+    )(made_users, made_items)
+    return new_users.reshape(users.shape), new_items.reshape(items.shape)
 
 
 def solution(mesh):

time: 93.2 us -> 81.4 us (0.87)
  the two profiles are of different devices: /device:TPU:69 before, /device:TPU:11 now
where the time goes in v2:
time: 81.4 us; the launch traced here: 81.3 us
  Pallas kernels  80 us (98%)
  between operations  1.29 us (2%)
    pallas_call x1, Pallas kernels, per_device(): pl.pallas_call(kernel, out_shape=(jax.ShapeDtypeStruct((UB, B, R), bf), j...  77.5 us
    pallas_call x1, Pallas kernels, per_device(): pl.pallas_call(deliver, out_shape=(jax.ShapeDtypeStruct((UB, B, R), bf),...  2.52 us

profile of v2, /device:TPU:11, one launch (start us, length us, event | category | flops | bytes accessed | tf_op | source)
XLA Modules:
  0.0 81.3 jit_solution(7091221833281963230)
XLA Ops:
  1.3 77.5 %round.1 = (bf16[32,128,256]{2,1,0:T(8,128)(2,1)}, bf16[4,128,256]{2,1,0:T(8,128)(2,1)}) custom-call(bf16[32,128,256]{2,1,0:T(8,128)(2,1)} %bitcast.4, bf16[4,128,256]{2,1,0:T(8,128)(2,1)} %bitcast.5, s32[1,8,16]{2,1,0:T(8,128)} %pairs.1, bf16[1,8,16,128,128]{4,3,2,1,0:T(8,128)(2,1)} %ratings.1, s32[1,8]{1,0:T(1,128)} %counts.1, s32[1,128]{1,0:T(1,128)} %ipairs.1, ...), custom_call_target="tpu_custom_call" | custom-call | tf_op jit(solution)/shard_map/round/pallas_call | solution.py:323
  78.7 2.5 %deliver.1 = (bf16[32,128,256]{2,1,0:T(8,128)(2,1)}, bf16[4,128,256]{2,1,0:T(8,128)(2,1)}) custom-call(bf16[32,128,256]{2,1,0:T(8,128)(2,1)} %get-tuple-element.6.made_users, bf16[4,128,256]{2,1,0:T(8,128)(2,1)} %get-tuple-element.7.made_items), custom_call_target="tpu_custom_call" | custom-call | tf_op jit(solution)/shard_map/deliver/pallas_call | solution.py:366

commit v3 on v2

--- a/solution.py
+++ b/solution.py
@@ -18,8 +18,11 @@
 NS = 8
 CAP = 16
 NSLOT = NS * CAP
-VMEM = 62 * 2**20
-PIECES = 4
+VMEM = 61 * 2**20
+GROUP = 4
+EARLY = 2
+SENDS = ((4, 3, 5, 2, 6, 1, 7), (4, 3, 5, 2, 6, 1, 7))
+TAKES = ((4, 3, 5, 2, 6, 1, 7), (4, 3, 5, 2, 6, 1, 7))
 
 ORDER = ((0, 0), (0, 1), (0, 3), (1, 0), (0, 2), (1, 1), (1, 3), (1, 2))
 
@@ -34,11 +37,11 @@
 
 def kernel(
     users, items, pairs, ratings, counts, ipairs, iratings, icount,
-    new_users, new_items,
+    nu_v, ni_v,
     h00, h01, h02, h03, h10, h11, h12, h13,
-    users_v, ur_v, ir_v, terms, nu_v, recv, acc, ni_v,
+    users_v, ur_v, ir_v, terms, recv, acc,
     pairs_s, counts_s, icount_s, pairs_v, ipairs_v, tab_v, tab_s,
-    lsem, ursem, gs, gr, ss, rs, osem, token, entered,
+    lsem, ursem, gs, gr, ss, rs, token, entered,
 ):
     blk = lax.axis_index("blk")
     wide = lax.axis_index("wide")
@@ -55,14 +58,18 @@
     across = (lax.rem(blk + 4, 8), wide)
 
     def partner(t, sign):
-        d = lax.div(t, 4)
-        dz = jnp.where(lax.rem(d, 2) == 0, lax.div(d, 2) + 1, 8 - 1 - lax.div(d, 2))
-        dz = jnp.where(t >= 28, 0, dz)
-        e = jnp.where(t >= 28, t - 27, lax.rem(t, 4))
-        zz = lax.rem(z + 8 + sign * dz, 8)
+        dz = lax.rem(lax.div(t, 4) + 1, 8)
+        e = lax.rem(t, 4)
         xx = lax.rem(xl + lax.div(e, 2), 2)
         cc = lax.rem(core + lax.rem(e, 2), 2)
+        zz = lax.rem(z + 8 + sign * dz, 8)
         return xx * 16 + zz * 2 + cc
+
+    def slot(n, order):
+        dz = 0
+        for m in range(7):
+            dz = jnp.where(n == m, jnp.where(z < 4, order[0][m], order[1][m]), dz)
+        return (dz - 1) * 4
 
     place = z
     below = xl * 16 + lax.rem(z + 7, 8) * 2 + core
@@ -93,13 +100,12 @@
     ]
     for copy in local:
         copy.start()
-    rating_copies = []
-    for j, (fx, dy) in enumerate(ORDER):
-        copy = pltpu.make_async_copy(ratings.at[0, slice_of(fx, dy)], ur_v.at[j], ursem.at[j])
-        copy.start()
-        rating_copies.append(copy)
+    rating_copies = [
+        pltpu.make_async_copy(ratings.at[0, slice_of(fx, dy)], ur_v.at[j], ursem.at[j])
+        for j, (fx, dy) in enumerate(ORDER)
+    ]
+    rating_copies[0].start()
     irating_copy = pltpu.make_async_copy(iratings.at[0], ir_v.at[pl.ds(0, NSLOT)], lsem.at[7])
-    irating_copy.start()
 
     pl.semaphore_wait(barrier, 6 + jnp.where(place < 7, 1, 0))
 
@@ -121,6 +127,8 @@
     go(3, items, h10, hi, across)
     go(4, items, h01, hi, up)
     go(5, items, h03, lo, down)
+    for copy in rating_copies[1:]:
+        copy.start()
 
     @pl.when(place > 0)
     def _():
@@ -172,9 +180,8 @@
         local[n].wait()
     tab_copy.wait()
 
-    STEP = 8
-
     def work(j):
+        STEP = CAP if j == NS - 1 else 8
         fx, dy = ORDER[j]
         cols_ref = held[(fx, dy)]
         s = slice_of(fx, dy)
@@ -216,6 +223,7 @@
     hops[5].wait_recv()
     work(2)
     work(3)
+    irating_copy.start()
     hops[6].wait_recv()
     hops[8].wait_recv()
     work(4)
@@ -247,20 +255,22 @@
             device_id=(blk, u), device_id_type=MESH,
         )
 
-    def send_out(t, carry):
+    def send_out(n, carry):
+        first = slot(n, SENDS)
+        for e in range(GROUP):
+            update(partner(first + e, 1))
+            relay(first + e).start()
+        return carry
+
+    lax.fori_loop(0, EARLY, send_out, 0)
+    for t in range(UB - GROUP + 1, UB):
         update(partner(t, 1))
         relay(t).start()
-        return carry
-
-    lax.fori_loop(0, UB - 1, send_out, 0)
+    lax.fori_loop(EARLY, UB // GROUP - 1, send_out, 0)
     update(wide)
-    recv[UB - 1] = nu_v[wide]
-    users_out = pltpu.make_async_copy(nu_v, new_users, osem.at[0])
-    users_out.start()
+    recv[UB - GROUP] = nu_v[wide]
     irating_copy.wait()
     acc[...] = jnp.zeros_like(acc)
-
-    GROUP = 4
 
     def absorb(t, owners):
         some = recv[pl.ds(t, GROUP)].reshape(GROUP * B, R)
@@ -271,22 +281,21 @@
             errs.append(jnp.where(rate != 0, rate - guess[i * B : (i + 1) * B], 0.0).astype(jnp.bfloat16))
         acc[...] += nn(jnp.concatenate(errs, axis=0), some).reshape(IB, B, R)
 
-    def take(q, carry):
-        t = q * GROUP
+    def take(n, carry):
+        t = slot(n, TAKES)
         for e in range(GROUP):
             relay(t + e).wait_recv()
         absorb(t, [partner(t + e, -1) for e in range(GROUP)])
         return carry
 
-    lax.fori_loop(0, UB // GROUP - 1, take, 0)
+    lax.fori_loop(0, EARLY, take, 0)
     t = UB - GROUP
-    for e in range(GROUP - 1):
+    for e in range(1, GROUP):
         relay(t + e).wait_recv()
-    absorb(t, [partner(t + e, -1) for e in range(GROUP - 1)] + [wide])
+    absorb(t, [wide] + [partner(t + e, -1) for e in range(1, GROUP)])
+    lax.fori_loop(EARLY, UB // GROUP - 1, take, 0)
     old = h00[...].astype(jnp.float32)
     ni_v[...] = (old + item_rate * (acc[...] - shrink * old)).astype(jnp.bfloat16)
-    items_out = pltpu.make_async_copy(ni_v, new_items, osem.at[1])
-    items_out.start()
 
     for n in hops:
         hops[n].wait_send()
@@ -295,39 +304,22 @@
         relay(t).wait_send()
         return carry
 
-    lax.fori_loop(0, UB - 1, sent, 0)
-    users_out.wait()
-    items_out.wait()
-
-
-def deliver(made_users, made_items, new_users, new_items, held_users, held_items, insem, outsem):
-    parts = [(made_items, held_items, new_items)]
-    for n in range(PIECES):
-        part = pl.ds(n * (UB // PIECES), UB // PIECES)
-        parts.append((made_users.at[part], held_users.at[part], new_users.at[part]))
-    reads = [pltpu.make_async_copy(a, b, insem.at[n]) for n, (a, b, c) in enumerate(parts)]
-    writes = [pltpu.make_async_copy(b, c, outsem.at[n]) for n, (a, b, c) in enumerate(parts)]
-    for copy in reads:
-        copy.start()
-    for read, write in zip(reads, writes):
-        read.wait()
-        write.start()
-    for copy in writes:
-        copy.wait()
+    lax.fori_loop(0, UB - GROUP, sent, 0)
+    lax.fori_loop(UB - GROUP + 1, UB, sent, 0)
 
 
 def per_device(
     users, items, user_pairs, user_ratings, user_counts, item_pairs, item_ratings, live_item_counts
 ):
     bf, f32, i32 = jnp.bfloat16, jnp.float32, jnp.int32
-    made_users, made_items = pl.pallas_call(
+    new_users, new_items = pl.pallas_call(
         kernel,
         out_shape=(
-            jax.ShapeDtypeStruct((UB, B, R), bf),
-            jax.ShapeDtypeStruct((IB, B, R), bf),
+            pltpu.VMEM((UB, B, R), bf),
+            pltpu.VMEM((IB, B, R), bf),
         ),
         in_specs=[pl.BlockSpec(memory_space=pl.ANY)] * 8,
-        out_specs=(pl.BlockSpec(memory_space=pl.ANY), pl.BlockSpec(memory_space=pl.ANY)),
+        out_specs=(pl.BlockSpec(memory_space=pltpu.VMEM), pl.BlockSpec(memory_space=pltpu.VMEM)),
         scratch_shapes=[pltpu.VMEM((IB, B, R), bf)] * 8
         + [
             pltpu.VMEM((UB, B, R), bf),
@@ -335,9 +327,7 @@
             pltpu.VMEM((NSLOT + 1, B, B), bf),
             pltpu.VMEM((NSLOT + 1, B, R), f32),
             pltpu.VMEM((UB, B, R), bf),
-            pltpu.VMEM((UB, B, R), bf),
             pltpu.VMEM((IB, B, R), f32),
-            pltpu.VMEM((IB, B, R), bf),
             pltpu.SMEM((1, NS, CAP), i32),
             pltpu.SMEM((1, NS), i32),
             pltpu.SMEM((1,), i32),
@@ -349,9 +339,8 @@
             pltpu.SemaphoreType.DMA((NS,)),
             pltpu.SemaphoreType.DMA((14,)),
             pltpu.SemaphoreType.DMA((14,)),
-            pltpu.SemaphoreType.DMA((UB - 1,)),
-            pltpu.SemaphoreType.DMA((UB - 1,)),
-            pltpu.SemaphoreType.DMA((2,)),
+            pltpu.SemaphoreType.DMA((UB,)),
+            pltpu.SemaphoreType.DMA((UB,)),
             pltpu.SemaphoreType.REGULAR,
             pltpu.SemaphoreType.REGULAR,
         ],
@@ -363,23 +352,6 @@
         users.reshape(UB, B, R), items.reshape(IB, B, R),
         user_pairs, user_ratings, user_counts, item_pairs, item_ratings, live_item_counts,
     )
-    new_users, new_items = pl.pallas_call(
-        deliver,
-        out_shape=(
-            jax.ShapeDtypeStruct((UB, B, R), bf),
-            jax.ShapeDtypeStruct((IB, B, R), bf),
-        ),
-        in_specs=[pl.BlockSpec(memory_space=pl.ANY)] * 2,
-        out_specs=(pl.BlockSpec(memory_space=pl.ANY), pl.BlockSpec(memory_space=pl.ANY)),
-        scratch_shapes=[
-            pltpu.VMEM((UB, B, R), bf),
-            pltpu.VMEM((IB, B, R), bf),
-            pltpu.SemaphoreType.DMA((PIECES + 1,)),
-            pltpu.SemaphoreType.DMA((PIECES + 1,)),
-        ],
-        compiler_params=pltpu.CompilerParams(vmem_limit_bytes=VMEM),
-        name="deliver",
-    )(made_users, made_items)
     return new_users.reshape(users.shape), new_items.reshape(items.shape)
 
 

time: 81.4 us -> 78.7 us (0.967); the launches traced: 81.3 us -> 77.6 us
  Pallas kernels: 80 us -> 74.3 us
  local copies, waits for them, and re-layouts: 0 us -> 2.02 us
    pallas_call x2 -> x1, Pallas kernels: 80 us -> 74.3 us  [per_device(): pl.pallas_call(kernel, out_shape=(pltpu.VMEM((UB, B, R), bf), pltpu.VMEM(...]
    unnamed x0 -> x2, local copies, waits for them, and re-layouts: none -> 2.02 us
where the time goes in v3:
time: 78.7 us; the launch traced here: 77.6 us
  Pallas kernels  74.3 us (94%)
  local copies, waits for them, and re-layouts  2.02 us (3%)
  between operations  1.29 us (2%)
    pallas_call x1, Pallas kernels, per_device(): pl.pallas_call(kernel, out_shape=(pltpu.VMEM((UB, B, R), bf), pltpu.VMEM(...  74.3 us
    unnamed x2, local copies, waits for them, and re-layouts  2.02 us

profile of v3, /device:TPU:11, one launch (start us, length us, event | category | flops | bytes accessed | tf_op | source)
XLA Modules:
  0.0 77.6 jit_solution(6188833017229671005)
XLA Ops:
  1.3 74.3 %round.1 = (bf16[32,128,256]{2,1,0:T(8,128)(2,1)S(1)}, bf16[4,128,256]{2,1,0:T(8,128)(2,1)S(1)}) custom-call(bf16[32,128,256]{2,1,0:T(8,128)(2,1)} %bitcast.6, bf16[4,128,256]{2,1,0:T(8,128)(2,1)} %bitcast.7, s32[1,8,16]{2,1,0:T(8,128)} %pairs.1, bf16[1,8,16,128,128]{4,3,2,1,0:T(8,128)(2,1)} %ratings.1, s32[1,8]{1,0:T(1,128)} %counts.1, s32[1,128]{1,0:T(1,128)} %ipairs.1, ...), custom_call_target="tpu_custom_call" | custom-call | tf_op jit(solution)/shard_map/round/pallas_call | solution.py:315
  75.6 1.3 %copy.12 = bf16[4096,256]{1,0:T(8,128)(2,1)} copy(bf16[4096,256]{1,0:T(8,128)(2,1)S(1)} %bitcast.4) | data formatting | bytes 4194304
  76.9 0.7 copy.13

commit v4 on v3

--- a/solution.py
+++ b/solution.py
@@ -19,9 +19,11 @@
 CAP = 16
 NSLOT = NS * CAP
 VMEM = 61 * 2**20
+LOCAL = 2**20
+PIECES = 4
 GROUP = 4
 EARLY = 2
-SENDS = ((4, 3, 5, 2, 6, 1, 7), (4, 3, 5, 2, 6, 1, 7))
+SENDS = ((3, 4, 5, 2, 6, 1, 7), (4, 3, 5, 2, 6, 1, 7))
 TAKES = ((4, 3, 5, 2, 6, 1, 7), (4, 3, 5, 2, 6, 1, 7))
 
 ORDER = ((0, 0), (0, 1), (0, 3), (1, 0), (0, 2), (1, 1), (1, 3), (1, 2))
@@ -308,11 +310,22 @@
     lax.fori_loop(UB - GROUP + 1, UB, sent, 0)
 
 
+def deliver(made_users, made_items, new_users, new_items, sem):
+    copies = [pltpu.make_async_copy(made_items, new_items, sem.at[PIECES])]
+    for n in range(PIECES):
+        part = pl.ds(n * (UB // PIECES), UB // PIECES)
+        copies.append(pltpu.make_async_copy(made_users.at[part], new_users.at[part], sem.at[n]))
+    for copy in copies:
+        copy.start()
+    for copy in copies:
+        copy.wait()
+
+
 def per_device(
     users, items, user_pairs, user_ratings, user_counts, item_pairs, item_ratings, live_item_counts
 ):
     bf, f32, i32 = jnp.bfloat16, jnp.float32, jnp.int32
-    new_users, new_items = pl.pallas_call(
+    made_users, made_items = pl.pallas_call(
         kernel,
         out_shape=(
             pltpu.VMEM((UB, B, R), bf),
@@ -352,6 +365,18 @@
         users.reshape(UB, B, R), items.reshape(IB, B, R),
         user_pairs, user_ratings, user_counts, item_pairs, item_ratings, live_item_counts,
     )
+    new_users, new_items = pl.pallas_call(
+        deliver,
+        out_shape=(
+            jax.ShapeDtypeStruct((UB, B, R), bf),
+            jax.ShapeDtypeStruct((IB, B, R), bf),
+        ),
+        in_specs=[pl.BlockSpec(memory_space=pl.ANY)] * 2,
+        out_specs=(pl.BlockSpec(memory_space=pl.ANY), pl.BlockSpec(memory_space=pl.ANY)),
+        scratch_shapes=[pltpu.SemaphoreType.DMA((PIECES + 1,))],
+        compiler_params=pltpu.CompilerParams(vmem_limit_bytes=LOCAL),
+        name="deliver",
+    )(made_users, made_items)
     return new_users.reshape(users.shape), new_items.reshape(items.shape)
 
 

time: 78.7 us -> 78.1 us (level)
  local copies, waits for them, and re-layouts: 2.02 us -> 0 us
  Pallas kernels: 74.3 us -> 75.4 us
    unnamed x2 -> x0, local copies, waits for them, and re-layouts: 2.02 us -> none
    pallas_call x0 -> x1, Pallas kernels: none -> 1.44 us  [per_device(): pl.pallas_call(deliver, out_shape=(jax.ShapeDtypeStruct((UB, B, R), bf),...]
where the time goes in v4:
time: 78.1 us; the launch traced here: 76.7 us
  Pallas kernels  75.4 us (97%)
  between operations  1.29 us (2%)
    pallas_call x1, Pallas kernels, per_device(): pl.pallas_call(kernel, out_shape=(pltpu.VMEM((UB, B, R), bf), pltpu.VMEM(...  74 us

profile of v4, /device:TPU:11, one launch (start us, length us, event | category | flops | bytes accessed | tf_op | source)
XLA Modules:
  0.0 76.7 jit_solution(12118405011855531312)
XLA Ops:
  1.3 74.0 %round.1 = (bf16[32,128,256]{2,1,0:T(8,128)(2,1)S(1)}, bf16[4,128,256]{2,1,0:T(8,128)(2,1)S(1)}) custom-call(bf16[32,128,256]{2,1,0:T(8,128)(2,1)} %bitcast.4, bf16[4,128,256]{2,1,0:T(8,128)(2,1)} %bitcast.5, s32[1,8,16]{2,1,0:T(8,128)} %pairs.1, bf16[1,8,16,128,128]{4,3,2,1,0:T(8,128)(2,1)} %ratings.1, s32[1,8]{1,0:T(1,128)} %counts.1, s32[1,128]{1,0:T(1,128)} %ipairs.1, ...), custom_call_target="tpu_custom_call" | custom-call | tf_op jit(solution)/shard_map/round/pallas_call | solution.py:328
  75.3 1.4 %deliver.1 = (bf16[32,128,256]{2,1,0:T(8,128)(2,1)}, bf16[4,128,256]{2,1,0:T(8,128)(2,1)}) custom-call(bf16[32,128,256]{2,1,0:T(8,128)(2,1)S(1)} %get-tuple-element.6.made_users, bf16[4,128,256]{2,1,0:T(8,128)(2,1)S(1)} %get-tuple-element.7.made_items), custom_call_target="tpu_custom_call" | custom-call | tf_op jit(solution)/shard_map/deliver/pallas_call | solution.py:368
